TPU v7x, 32 devices: a whole 2x2x4 slice. The times are simulated.
32 devices in a mesh: ctx: 8 (over z, y), mp: 4 (over x, core).
Axes of the slice: x: 2, y: 2, z: 4, core: 2. Of those that a mesh axis runs over, the one named last changes fastest.
Arguments:
- queries: bfloat16 [2, 1536, 5120], P(None, 'ctx', 'mp'), may hold values from -24 to 24
- cache_keys: bfloat16 [1536, 5120], P(('ctx', 'mp')), may hold values from -26 to 26
- cache_values: bfloat16 [1536, 5120], P(('ctx', 'mp')), may hold values from -6 to 6
- douts: bfloat16 [2, 1536, 5120], P(None, 'ctx', 'mp'), may hold values from -6 to 6
- reads: int32 [8, 24], P('ctx'), may hold values from -1 to 95, as said below
Outputs:
- attn_out: bfloat16 [2, 1536, 5120], P(None, 'ctx', 'mp')
- d_queries: bfloat16 [2, 1536, 5120], P(None, 'ctx', 'mp')
- d_cache_keys: float32 [1536, 5120], P(('ctx', 'mp'))
- d_cache_values: float32 [1536, 5120], P(('ctx', 'mp'))
Inputs may be any that keep to these rules, and one draw needn't show every extreme that they name: Row c names, in rising order, the blocks that stretch c reads, then -1 in the remaining slots. Every named block ends at or before stretch c's last position. Block 0 is named in every row. Owner o holds blocks 3 * o to 3 * o + 2; a row names at most one block of an owner, and exactly one of each of the 4 owners of stretch c's own positions. Row c names min(24, 4 * (c + 1)) blocks.
All inputs are finite; a program needn't handle non-finite values.
Results may differ from a plain program's by a relative error of at most 0.017.
Values may be sent and summed in bfloat16 or wider, within the bound.
A program may use at most 256 MiB of HBM per device.

v0:
```python
import functools
import math

import jax
import jax.numpy as jnp
from jax import lax
from jax.experimental import pallas as pl
from jax.experimental.pallas import tpu as pltpu
from jax.sharding import PartitionSpec as P

HD = 128
BLK = 16
LANES = 128
MESH = pl.DeviceIdType.MESH
FAR = 1e9
LOW = -1e30


def rows_by(a, b):
    return lax.dot_general(a, b, (((1,), (1,)), ((), ())), preferred_element_type=jnp.float32)


def plain(a, b):
    return lax.dot_general(a, b, (((1,), (0,)), ((), ())), preferred_element_type=jnp.float32)


def over_rows(a, b):
    return lax.dot_general(a, b, (((0,), (0,)), ((), ())), preferred_element_type=jnp.float32)


def kernel(
    sizes,
    q_ref,
    k_ref,
    v_ref,
    do_ref,
    list_ref,
    o_ref,
    dq_ref,
    dk_ref,
    dv_ref,
    out_blocks,
    kv_blocks,
    grad_blocks,
    lists,
    hits,
    bias,
    list_send,
    list_recv,
    kv_send,
    kv_recv,
    grad_send,
    grad_recv,
):
    ctx_n, mp_n, chunks, width = sizes
    layers, tok, head_width = q_ref.shape
    per_owner = k_ref.shape[0] // BLK
    owners = ctx_n * mp_n
    keys = owners * BLK
    factor = 1.0 / math.sqrt(HD)
    my_c = lax.axis_index("ctx")
    my_m = lax.axis_index("mp")
    owner = my_c * mp_n + my_m

    def columns(m, ch):
        return pl.ds(pl.multiple_of(m * head_width + ch * width, LANES), width)

    def loop(low, high, body):
        def step(i, carry):
            body(i)
            return carry

        lax.fori_loop(low, high, step, 0)

    def wait_bytes(ref, sem):
        pltpu.make_async_copy(ref, ref, sem).wait()

    def clear(ch):
        kv_blocks[ch] = jnp.zeros(kv_blocks.shape[1:], kv_blocks.dtype)

    loop(0, chunks, clear)
    lists[...] = jnp.full(lists.shape, -1, jnp.int32)
    lists[my_c] = list_ref[...]

    barrier = pltpu.get_barrier_semaphore()

    def greet(t):
        @pl.when(t != owner)
        def _():
            pl.semaphore_signal(
                barrier, inc=1, device_id=(t // mp_n, t % mp_n), device_id_type=MESH
            )

    loop(0, owners, greet)
    pl.semaphore_wait(barrier, owners - 1)

    def send_list(c):
        pltpu.make_async_remote_copy(
            src_ref=list_ref,
            dst_ref=lists.at[my_c],
            send_sem=list_send.at[c],
            recv_sem=list_recv.at[my_c],
            device_id=(c, my_m),
            device_id_type=MESH,
        ).start()

    loop(0, my_c, send_list)

    named = list_ref[...].T[:, 0:1]
    lane = lax.broadcasted_iota(jnp.int32, (named.shape[0], keys), 1)
    first = (lane >> 4) * per_owner
    hit = (named >= first) & (named < first + per_owner)
    key_pos = jnp.sum(
        jnp.where(hit, (named * BLK + (lane & (BLK - 1))).astype(jnp.float32), 0.0),
        axis=0,
        keepdims=True,
    )
    live = jnp.sum(jnp.where(hit, 1.0, 0.0), axis=0, keepdims=True)
    key_pos = jnp.where(live > 0.5, key_pos, FAR)
    query_pos = (my_c * tok + lax.broadcasted_iota(jnp.int32, (tok, keys), 0)).astype(jnp.float32)
    bias[...] = jnp.where(key_pos <= query_pos, 0.0, LOW)

    loop(my_c + 1, ctx_n, lambda c: wait_bytes(lists.at[c], list_recv.at[c]))
    rows = lists[:, 0, :]
    for b in range(per_owner):
        found = jnp.sum(
            jnp.where(rows == owner * per_owner + b, 1.0, 0.0), axis=1, keepdims=True
        )
        hits[b] = jnp.broadcast_to(found, (ctx_n, width))

    def send_chunk(ch):
        def to_stretch(step):
            c = ctx_n - 1 - step
            wanted = [hits[b, pl.ds(c, 1), :] for b in range(per_owner)]
            for i in range(mp_n):
                m = lax.rem(my_m + i, mp_n)
                cols = columns(m, ch)
                for part, source in enumerate((k_ref, v_ref)):
                    picked = source[0:BLK, cols].astype(jnp.float32) * wanted[0]
                    for b in range(1, per_owner):
                        block = source[b * BLK : (b + 1) * BLK, cols].astype(jnp.float32)
                        picked = picked + block * wanted[b]
                    out_blocks[ch, c, m, part] = picked.astype(jnp.bfloat16)

                def away(m=m):
                    pltpu.make_async_remote_copy(
                        src_ref=out_blocks.at[ch, c, m],
                        dst_ref=kv_blocks.at[ch, :, owner],
                        send_sem=kv_send.at[ch, c],
                        recv_sem=kv_recv.at[ch, my_c],
                        device_id=(c, m),
                        device_id_type=MESH,
                    ).start()

                if i > 0:
                    away()
                else:
                    pl.when(c != my_c)(away)

                    @pl.when(c == my_c)
                    def _(m=m):
                        pltpu.make_async_copy(
                            out_blocks.at[ch, c, m],
                            kv_blocks.at[ch, :, owner],
                            kv_recv.at[ch, my_c],
                        ).start()

        loop(0, ctx_n - my_c, to_stretch)

    loop(0, chunks, send_chunk)

    def work_chunk(ch):
        loop(
            0,
            my_c + 1,
            lambda s: wait_bytes(
                kv_blocks.at[ch, :, pl.ds(s * mp_n, mp_n)], kv_recv.at[ch, s]
            ),
        )
        for h in range(width // HD):
            here = slice(h * HD, (h + 1) * HD)
            cols = pl.ds(pl.multiple_of(ch * width + h * HD, LANES), HD)
            key_rows = kv_blocks[ch, 0, :, :, here].reshape(keys, HD)
            value_rows = kv_blocks[ch, 1, :, :, here].reshape(keys, HD)
            query_rows = q_ref[:, :, cols].reshape(layers * tok, HD)
            dout_rows = do_ref[:, :, cols].reshape(layers * tok, HD)
            scores = rows_by(query_rows, key_rows) * factor
            scores = (scores.reshape(layers, tok, keys) + bias[...][None]).reshape(
                layers * tok, keys
            )
            raised = jnp.exp(scores - jnp.max(scores, axis=1, keepdims=True))
            probs = raised * (1.0 / jnp.sum(raised, axis=1, keepdims=True))
            probs_low = probs.astype(jnp.bfloat16)
            attended = plain(probs_low, value_rows).astype(jnp.bfloat16)
            delta = jnp.sum(
                dout_rows.astype(jnp.float32) * attended.astype(jnp.float32),
                axis=1,
                keepdims=True,
            )
            d_probs = rows_by(dout_rows, value_rows)
            d_scores = (probs * (d_probs - delta)).astype(jnp.bfloat16)
            o_ref[:, :, cols] = attended.reshape(layers, tok, HD)
            d_query = (plain(d_scores, key_rows) * factor).astype(jnp.bfloat16)
            dq_ref[:, :, cols] = d_query.reshape(layers, tok, HD)
            d_keys = (over_rows(d_scores, query_rows) * factor).astype(jnp.bfloat16)
            d_values = over_rows(probs_low, dout_rows).astype(jnp.bfloat16)
            kv_blocks[ch, 0, :, :, here] = d_keys.reshape(owners, BLK, HD)
            kv_blocks[ch, 1, :, :, here] = d_values.reshape(owners, BLK, HD)

        def to_owners(s):
            for i in range(mp_n):
                m = lax.rem(my_m + i, mp_n)

                def away(m=m):
                    pltpu.make_async_remote_copy(
                        src_ref=kv_blocks.at[ch, :, s * mp_n + m],
                        dst_ref=grad_blocks.at[ch, my_c, my_m],
                        send_sem=grad_send.at[ch, s],
                        recv_sem=grad_recv.at[ch, my_c],
                        device_id=(s, m),
                        device_id_type=MESH,
                    ).start()

                if i > 0:
                    away()
                else:
                    pl.when(s != my_c)(away)

                    @pl.when(s == my_c)
                    def _():
                        pltpu.make_async_copy(
                            kv_blocks.at[ch, :, owner],
                            grad_blocks.at[ch, my_c, my_m],
                            grad_recv.at[ch, my_c],
                        ).start()

        loop(0, my_c + 1, to_owners)

    loop(0, chunks, work_chunk)

    dk_ref[...] = jnp.zeros(dk_ref.shape, jnp.float32)
    dv_ref[...] = jnp.zeros(dv_ref.shape, jnp.float32)

    def absorb_chunk(ch):
        def from_stretch(c):
            wait_bytes(grad_blocks.at[ch, c], grad_recv.at[ch, c])
            wanted = [hits[b, pl.ds(c, 1), :] for b in range(per_owner)]
            for m in range(mp_n):
                cols = columns(m, ch)
                for part, target in enumerate((dk_ref, dv_ref)):
                    grad = grad_blocks[ch, c, m, part].astype(jnp.float32)
                    for b in range(per_owner):
                        target[b * BLK : (b + 1) * BLK, cols] += grad * wanted[b]

        loop(my_c, ctx_n, from_stretch)

    loop(0, chunks, absorb_chunk)

    loop(0, my_c, lambda c: wait_bytes(list_ref, list_send.at[c]))

    def finish(ch):
        loop(my_c + 1, ctx_n, lambda c: wait_bytes(out_blocks.at[ch, c], kv_send.at[ch, c]))
        wait_bytes(out_blocks.at[ch, my_c, pl.ds(0, mp_n - 1)], kv_send.at[ch, my_c])
        loop(
            0,
            my_c,
            lambda s: wait_bytes(
                kv_blocks.at[ch, :, pl.ds(s * mp_n, mp_n)], grad_send.at[ch, s]
            ),
        )
        wait_bytes(kv_blocks.at[ch, :, pl.ds(my_c * mp_n, mp_n - 1)], grad_send.at[ch, my_c])

    loop(0, chunks, finish)


def on_device(queries, cache_keys, cache_values, douts, reads):
    layers, tok, head_width = queries.shape
    kv_rows, full_width = cache_keys.shape
    ctx_n = lax.axis_size("ctx")
    mp_n = lax.axis_size("mp")
    per_owner = kv_rows // BLK
    owners = ctx_n * mp_n
    heads = head_width // HD
    per_chunk = 2 if heads % 2 == 0 else 1
    chunks = heads // per_chunk
    width = per_chunk * HD
    slots = reads.shape[1]
    padded = -(-slots // LANES) * LANES
    listed = jnp.pad(reads, ((0, 7), (0, padded - slots)), constant_values=-1)
    vmem = pl.BlockSpec(memory_space=pltpu.VMEM)
    dma = pltpu.SemaphoreType.DMA
    return pl.pallas_call(
        functools.partial(kernel, (ctx_n, mp_n, chunks, width)),
        out_shape=(
            jax.ShapeDtypeStruct(queries.shape, jnp.bfloat16),
            jax.ShapeDtypeStruct(queries.shape, jnp.bfloat16),
            jax.ShapeDtypeStruct(cache_keys.shape, jnp.float32),
            jax.ShapeDtypeStruct(cache_values.shape, jnp.float32),
        ),
        in_specs=[vmem] * 5,
        out_specs=(vmem,) * 4,
        scratch_shapes=[
            pltpu.VMEM((chunks, ctx_n, mp_n, 2, BLK, width), jnp.bfloat16),
            pltpu.VMEM((chunks, 2, owners, BLK, width), jnp.bfloat16),
            pltpu.VMEM((chunks, ctx_n, mp_n, 2, BLK, width), jnp.bfloat16),
            pltpu.VMEM((ctx_n, 8, padded), jnp.int32),
            pltpu.VMEM((per_owner, ctx_n, width), jnp.float32),
            pltpu.VMEM((tok, owners * BLK), jnp.float32),
            dma((ctx_n,)),
            dma((ctx_n,)),
            dma((chunks, ctx_n)),
            dma((chunks, ctx_n)),
            dma((chunks, ctx_n)),
            dma((chunks, ctx_n)),
        ],
        compiler_params=pltpu.CompilerParams(
            collective_id=0, has_side_effects=True, vmem_limit_bytes=60 * 1024 * 1024
        ),
    )(queries, cache_keys, cache_values, douts, listed)


def solution(mesh):
    return jax.shard_map(
        on_device,
        mesh=mesh,
        in_specs=(
            P(None, "ctx", "mp"),
            P(("ctx", "mp"), None),
            P(("ctx", "mp"), None),
            P(None, "ctx", "mp"),
            P("ctx", None),
        ),
        out_specs=(
            P(None, "ctx", "mp"),
            P(None, "ctx", "mp"),
            P(("ctx", "mp"), None),
            P(("ctx", "mp"), None),
        ),
        check_vma=False,
    )
```

profile of v0, /device:TPU:13, one launch (start us, length us, event | category | flops | bytes accessed | tf_op | source)
XLA Modules:
  0.0 106.1 jit_solution(2938028940453641878)
XLA Ops:
  0.6 1.3 %pad.4.list_ref = s32[8,128]{1,0:T(8,128)} pad(s32[1,24]{1,0:T(1,128)} %param.9, s32[]{:T(128)} %constant.0.clone.1), padding=0_7x0_104 | pad | bytes 4196 | tf_op jit(solution)/shard_map/jit(_pad)/pad | solution.py:289
  1.9 97.8 %shard_map.84 = (bf16[2,192,1280]{2,1,0:T(8,128)(2,1)}, bf16[2,192,1280]{2,1,0:T(8,128)(2,1)}, f32[48,5120]{1,0:T(8,128)}, f32[48,5120]{1,0:T(8,128)}) custom-call(bf16[2,192,1280]{2,1,0:T(8,128)(2,1)} %q_ref.1, bf16[48,5120]{1,0:T(8,128)(2,1)} %k_ref.1, bf16[48,5120]{1,0:T(8,128)(2,1)} %v_ref.1, bf16[2,192,1280]{2,1,0:T(8,128)(2,1)} %do_ref.1, ...), custom_call_target="tpu_custom_call" | custom-call | tf_op jit(solution)/shard_map/pallas_call | solution.py:292
  99.7 0.0 copy-start.2
  99.7 2.3 %copy.13 = bf16[2,192,1280]{2,1,0:T(8,128)(2,1)} copy(bf16[2,192,1280]{2,1,0:T(8,128)(2,1)} %get-tuple-element.8) | data formatting | bytes 1966080
  102.0 0.0 copy-done.2
  102.0 0.0 copy-start.1
  102.0 0.9 copy.14
  103.0 0.6 copy-done.1
  103.6 0.0 copy-start
  103.6 0.9 copy.15
  104.5 0.6 copy-done
  105.1 0.9 copy.16
Async XLA Ops:
  99.7 2.3 %copy-start.2 = (bf16[2,192,1280]{2,1,0:T(8,128)(2,1)S(1)}, bf16[2,192,1280]{2,1,0:T(8,128)(2,1)}, u32[]{:S(2)}) copy-start(bf16[2,192,1280]{2,1,0:T(8,128)(2,1)} %get-tuple-element.9) | copy-start | bytes 2949124
  102.0 1.6 %copy-start.1 = (f32[48,5120]{1,0:T(8,128)S(1)}, f32[48,5120]{1,0:T(8,128)}, u32[]{:S(2)}) copy-start(f32[48,5120]{1,0:T(8,128)} %get-tuple-element.10) | copy-start | bytes 2949124
  103.6 1.6 %copy-start = (f32[48,5120]{1,0:T(8,128)S(1)}, f32[48,5120]{1,0:T(8,128)}, u32[]{:S(2)}) copy-start(f32[48,5120]{1,0:T(8,128)} %get-tuple-element.11) | copy-start | bytes 2949124
where the time goes:
time: 106 us
  Pallas kernels  97.8 us (92%)
  local copies, waits for them, and re-layouts  7.6 us (7%)
    pallas_call x1, Pallas kernels, on_device(): pl.pallas_call(functools.partial(kernel, (ctx_n, mp_n, chunks, width)), o...  97.8 us
    unnamed x10, local copies, waits for them, and re-layouts  6.35 us

commit v1 on v0

--- a/solution.py
+++ b/solution.py
@@ -34,7 +34,7 @@
     k_ref,
     v_ref,
     do_ref,
-    list_ref,
+    reads_ref,
     o_ref,
     dq_ref,
     dk_ref,
@@ -42,6 +42,7 @@
     out_blocks,
     kv_blocks,
     grad_blocks,
+    list_ref,
     lists,
     hits,
     bias,
@@ -79,6 +80,8 @@
         kv_blocks[ch] = jnp.zeros(kv_blocks.shape[1:], kv_blocks.dtype)
 
     loop(0, chunks, clear)
+    list_ref[...] = jnp.full(list_ref.shape, -1, jnp.int32)
+    list_ref[0:1, 0 : reads_ref.shape[1]] = reads_ref[...]
     lists[...] = jnp.full(lists.shape, -1, jnp.int32)
     lists[my_c] = list_ref[...]
 
@@ -145,7 +148,7 @@
                 def away(m=m):
                     pltpu.make_async_remote_copy(
                         src_ref=out_blocks.at[ch, c, m],
-                        dst_ref=kv_blocks.at[ch, :, owner],
+                        dst_ref=kv_blocks.at[ch, owner],
                         send_sem=kv_send.at[ch, c],
                         recv_sem=kv_recv.at[ch, my_c],
                         device_id=(c, m),
@@ -161,7 +164,7 @@
                     def _(m=m):
                         pltpu.make_async_copy(
                             out_blocks.at[ch, c, m],
-                            kv_blocks.at[ch, :, owner],
+                            kv_blocks.at[ch, owner],
                             kv_recv.at[ch, my_c],
                         ).start()
 
@@ -174,14 +177,14 @@
             0,
             my_c + 1,
             lambda s: wait_bytes(
-                kv_blocks.at[ch, :, pl.ds(s * mp_n, mp_n)], kv_recv.at[ch, s]
+                kv_blocks.at[ch, pl.ds(s * mp_n, mp_n)], kv_recv.at[ch, s]
             ),
         )
         for h in range(width // HD):
             here = slice(h * HD, (h + 1) * HD)
             cols = pl.ds(pl.multiple_of(ch * width + h * HD, LANES), HD)
-            key_rows = kv_blocks[ch, 0, :, :, here].reshape(keys, HD)
-            value_rows = kv_blocks[ch, 1, :, :, here].reshape(keys, HD)
+            key_rows = kv_blocks[ch, :, 0, :, here].reshape(keys, HD)
+            value_rows = kv_blocks[ch, :, 1, :, here].reshape(keys, HD)
             query_rows = q_ref[:, :, cols].reshape(layers * tok, HD)
             dout_rows = do_ref[:, :, cols].reshape(layers * tok, HD)
             scores = rows_by(query_rows, key_rows) * factor
@@ -204,8 +207,8 @@
             dq_ref[:, :, cols] = d_query.reshape(layers, tok, HD)
             d_keys = (over_rows(d_scores, query_rows) * factor).astype(jnp.bfloat16)
             d_values = over_rows(probs_low, dout_rows).astype(jnp.bfloat16)
-            kv_blocks[ch, 0, :, :, here] = d_keys.reshape(owners, BLK, HD)
-            kv_blocks[ch, 1, :, :, here] = d_values.reshape(owners, BLK, HD)
+            kv_blocks[ch, :, 0, :, here] = d_keys.reshape(owners, BLK, HD)
+            kv_blocks[ch, :, 1, :, here] = d_values.reshape(owners, BLK, HD)
 
         def to_owners(s):
             for i in range(mp_n):
@@ -213,7 +216,7 @@
 
                 def away(m=m):
                     pltpu.make_async_remote_copy(
-                        src_ref=kv_blocks.at[ch, :, s * mp_n + m],
+                        src_ref=kv_blocks.at[ch, s * mp_n + m],
                         dst_ref=grad_blocks.at[ch, my_c, my_m],
                         send_sem=grad_send.at[ch, s],
                         recv_sem=grad_recv.at[ch, my_c],
@@ -229,7 +232,7 @@
                     @pl.when(s == my_c)
                     def _():
                         pltpu.make_async_copy(
-                            kv_blocks.at[ch, :, owner],
+                            kv_blocks.at[ch, owner],
                             grad_blocks.at[ch, my_c, my_m],
                             grad_recv.at[ch, my_c],
                         ).start()
@@ -265,12 +268,25 @@
             0,
             my_c,
             lambda s: wait_bytes(
-                kv_blocks.at[ch, :, pl.ds(s * mp_n, mp_n)], grad_send.at[ch, s]
+                kv_blocks.at[ch, pl.ds(s * mp_n, mp_n)], grad_send.at[ch, s]
             ),
         )
-        wait_bytes(kv_blocks.at[ch, :, pl.ds(my_c * mp_n, mp_n - 1)], grad_send.at[ch, my_c])
+        wait_bytes(kv_blocks.at[ch, pl.ds(my_c * mp_n, mp_n - 1)], grad_send.at[ch, my_c])
 
     loop(0, chunks, finish)
+
+
+def store(*refs):
+    half = len(refs) // 2
+    sems, refs = refs[-1], refs[:-1]
+    copies = [
+        pltpu.make_async_copy(a, b, sems.at[i])
+        for i, (a, b) in enumerate(zip(refs[:half], refs[half:]))
+    ]
+    for copy in copies:
+        copy.start()
+    for copy in copies:
+        copy.wait()
 
 
 def on_device(queries, cache_keys, cache_values, douts, reads):
@@ -281,15 +297,13 @@
     per_owner = kv_rows // BLK
     owners = ctx_n * mp_n
     heads = head_width // HD
-    per_chunk = 2 if heads % 2 == 0 else 1
-    chunks = heads // per_chunk
-    width = per_chunk * HD
+    chunks = heads
+    width = HD
     slots = reads.shape[1]
     padded = -(-slots // LANES) * LANES
-    listed = jnp.pad(reads, ((0, 7), (0, padded - slots)), constant_values=-1)
     vmem = pl.BlockSpec(memory_space=pltpu.VMEM)
     dma = pltpu.SemaphoreType.DMA
-    return pl.pallas_call(
+    results = pl.pallas_call(
         functools.partial(kernel, (ctx_n, mp_n, chunks, width)),
         out_shape=(
             jax.ShapeDtypeStruct(queries.shape, jnp.bfloat16),
@@ -301,8 +315,9 @@
         out_specs=(vmem,) * 4,
         scratch_shapes=[
             pltpu.VMEM((chunks, ctx_n, mp_n, 2, BLK, width), jnp.bfloat16),
-            pltpu.VMEM((chunks, 2, owners, BLK, width), jnp.bfloat16),
+            pltpu.VMEM((chunks, owners, 2, BLK, width), jnp.bfloat16),
             pltpu.VMEM((chunks, ctx_n, mp_n, 2, BLK, width), jnp.bfloat16),
+            pltpu.VMEM((8, padded), jnp.int32),
             pltpu.VMEM((ctx_n, 8, padded), jnp.int32),
             pltpu.VMEM((per_owner, ctx_n, width), jnp.float32),
             pltpu.VMEM((tok, owners * BLK), jnp.float32),
@@ -316,7 +331,16 @@
         compiler_params=pltpu.CompilerParams(
             collective_id=0, has_side_effects=True, vmem_limit_bytes=60 * 1024 * 1024
         ),
-    )(queries, cache_keys, cache_values, douts, listed)
+    )(queries, cache_keys, cache_values, douts, reads)
+    anywhere = pl.BlockSpec(memory_space=pl.ANY)
+    return pl.pallas_call(
+        store,
+        out_shape=[jax.ShapeDtypeStruct(r.shape, r.dtype) for r in results],
+        in_specs=[vmem] * 4,
+        out_specs=[anywhere] * 4,
+        scratch_shapes=[dma((4,))],
+        compiler_params=pltpu.CompilerParams(vmem_limit_bytes=16 * 1024 * 1024),
+    )(*results)
 
 
 def solution(mesh):

time: 106 us -> 104 us (0.981)
  local copies, waits for them, and re-layouts: 7.6 us -> 4.8 us
    pallas_call x0 -> x1, Pallas kernels: none -> 1.95 us  [on_device(): pl.pallas_call(store, out_shape=[jax.ShapeDtypeStruct(r.shape, r.dtype) f...]
    unnamed x10 -> x8, local copies, waits for them, and re-layouts: 6.35 us -> 4.8 us
    pallas_call x1, Pallas kernels: 97.8 us -> 96.4 us  [on_device(): pl.pallas_call(functools.partial(kernel, (ctx_n, mp_n, chunks, width)), o...]
    pad x1 -> x0, local copies, waits for them, and re-layouts: 1.25 us -> none  [on_device(): listed = jnp.pad(reads, ((0, 7), (0, padded - slots)), constant_values=-1)]
where the time goes in v1:
time: 104 us
  Pallas kernels  98.3 us (95%)
  local copies, waits for them, and re-layouts  4.8 us (5%)
    pallas_call x1, Pallas kernels, on_device(): pl.pallas_call(functools.partial(kernel, (ctx_n, mp_n, chunks, width)), o...  96.4 us
    unnamed x8, local copies, waits for them, and re-layouts  4.8 us

profile of v1, /device:TPU:13, one launch (start us, length us, event | category | flops | bytes accessed | tf_op | source)
XLA Modules:
  0.0 103.8 jit_solution(17890900686452025902)
XLA Ops:
  0.6 96.4 %shard_map.84 = (bf16[2,192,1280]{2,1,0:T(8,128)(2,1)}, bf16[2,192,1280]{2,1,0:T(8,128)(2,1)}, f32[48,5120]{1,0:T(8,128)}, f32[48,5120]{1,0:T(8,128)}) custom-call(bf16[2,192,1280]{2,1,0:T(8,128)(2,1)} %q_ref.1, bf16[48,5120]{1,0:T(8,128)(2,1)} %k_ref.1, bf16[48,5120]{1,0:T(8,128)(2,1)} %v_ref.1, bf16[2,192,1280]{2,1,0:T(8,128)(2,1)} %do_ref.1, ...), custom_call_target="tpu_custom_call" | custom-call | tf_op jit(solution)/shard_map/pallas_call | solution.py:306
  97.0 0.0 copy-start
  97.0 1.2 %copy-done = bf16[2,192,1280]{2,1,0:T(8,128)(2,1)S(1)} copy-done((bf16[2,192,1280]{2,1,0:T(8,128)(2,1)S(1)}, bf16[2,192,1280]{2,1,0:T(8,128)(2,1)}, u32[]{:S(2)}) %copy-start) | copy-done | bytes 983064
  98.2 0.0 copy-start.1
  98.2 1.2 %copy-done.1 = bf16[2,192,1280]{2,1,0:T(8,128)(2,1)S(1)} copy-done((bf16[2,192,1280]{2,1,0:T(8,128)(2,1)S(1)}, bf16[2,192,1280]{2,1,0:T(8,128)(2,1)}, u32[]{:S(2)}) %copy-start.1) | copy-done | bytes 983064
  99.4 0.0 copy-start.2
  99.4 1.2 %copy-done.2 = f32[48,5120]{1,0:T(8,128)S(1)} copy-done((f32[48,5120]{1,0:T(8,128)S(1)}, f32[48,5120]{1,0:T(8,128)}, u32[]{:S(2)}) %copy-start.2) | copy-done | bytes 983064
  100.6 0.0 copy-start.3
  100.6 1.2 %copy-done.3 = f32[48,5120]{1,0:T(8,128)S(1)} copy-done((f32[48,5120]{1,0:T(8,128)S(1)}, f32[48,5120]{1,0:T(8,128)}, u32[]{:S(2)}) %copy-start.3) | copy-done | bytes 983064
  101.8 1.9 %shard_map.85 = (bf16[2,192,1280]{2,1,0:T(8,128)(2,1)}, bf16[2,192,1280]{2,1,0:T(8,128)(2,1)}, f32[48,5120]{1,0:T(8,128)}, f32[48,5120]{1,0:T(8,128)}) custom-call(bf16[2,192,1280]{2,1,0:T(8,128)(2,1)S(1)} %copy-done, bf16[2,192,1280]{2,1,0:T(8,128)(2,1)S(1)} %copy-done.1, f32[48,5120]{1,0:T(8,128)S(1)} %copy-done.2, f32[48,5120]{1,0:T(8,128)S(1)} %copy-done.3), custom_call_target="tpu_custom_call" | custom-call | tf_op jit(solution)/shard_map/pallas_call | solution.py:336
Async XLA Ops:
  97.0 1.2 %copy-start = (bf16[2,192,1280]{2,1,0:T(8,128)(2,1)S(1)}, bf16[2,192,1280]{2,1,0:T(8,128)(2,1)}, u32[]{:S(2)}) copy-start(bf16[2,192,1280]{2,1,0:T(8,128)(2,1)} %get-tuple-element.8.refs_0_) | copy-start | bytes 2949124
  98.2 1.2 %copy-start.1 = (bf16[2,192,1280]{2,1,0:T(8,128)(2,1)S(1)}, bf16[2,192,1280]{2,1,0:T(8,128)(2,1)}, u32[]{:S(2)}) copy-start(bf16[2,192,1280]{2,1,0:T(8,128)(2,1)} %get-tuple-element.9.refs_1_) | copy-start | bytes 2949124
  99.4 1.2 %copy-start.2 = (f32[48,5120]{1,0:T(8,128)S(1)}, f32[48,5120]{1,0:T(8,128)}, u32[]{:S(2)}) copy-start(f32[48,5120]{1,0:T(8,128)} %get-tuple-element.10.refs_2_) | copy-start | bytes 2949124
  100.6 1.2 %copy-start.3 = (f32[48,5120]{1,0:T(8,128)S(1)}, f32[48,5120]{1,0:T(8,128)}, u32[]{:S(2)}) copy-start(f32[48,5120]{1,0:T(8,128)} %get-tuple-element.11.refs_3_) | copy-start | bytes 2949124
